TPU v7x, 32 devices: a whole 2x2x4 slice. The times are simulated.
32 devices in a mesh: runs: 2 (over y), pts: 4 (over z), tm: 2 (over x), rep: 2 (over core).
Axes of the slice: x: 2, y: 2, z: 4, core: 2. Of those that a mesh axis runs over, the one named last changes fastest.
Arguments:
- wind_speed: bfloat16 [256, 1024], P(('runs', 'pts'), 'tm'), parts along dimension 0, may hold values from -6 to 6
- span_of_point: int32 [8192], P('pts'), may hold values from 0 to 127, as said below
- drag_factor: float32 [8192], P('pts'), may hold values from 0.3 to 3
- mode_shapes: bfloat16 [8192, 4096], P('pts', 'rep'), may hold values from -0.09375 to 0.09375
- damping: float32 [4096], P('rep'), as said below
- turning: float32 [4096], P('rep'), may hold values from 0.05 to 2.5
- prior_state: float32 [4, 4096], P('runs', 'rep'), parts along dimension 0, may hold values from -6 to 6
- recovery: bfloat16 [4096, 2048], P('rep', 'pts'), may hold values from -0.125 to 0.125
Outputs:
- stress: bfloat16 [2048, 2048], P(('runs', 'tm'), ('pts', 'rep')), parts along dimension 0
There are 2 independent parts, one for each index of `runs`. A program takes and returns all parts, laid end to end along the dimension named above; an argument that names none is the same for every part. Nothing has to cross between parts.
Inputs may be any that keep to these rules, and one draw needn't show every extreme that they name: `span_of_point`: load points lie in the spans of the same index of pts, 32 spans to an index, and their span never falls along the points. `damping`: every decay rate is positive and at most 1/30.
All inputs are finite; a program needn't handle non-finite values.
Results may differ from a plain program's by a relative error of at most 0.015.
Values may be sent and summed in bfloat16 or wider, within the bound.
A program may use at most 64 MiB of HBM per device.

v0:
```python
import jax
import jax.numpy as jnp
from jax import lax
from jax.sharding import PartitionSpec as P


def passed_along(shard, axis, by):
    length = lax.axis_size(axis)
    pairs = [(i, i + by) for i in range(length) if 0 <= i + by < length]
    return lax.ppermute(shard, axis, pairs)


def running_sum(values, triangle_bf):
    high_part = values.astype(jnp.bfloat16)
    low_part = (values - high_part.astype(jnp.float32)).astype(jnp.bfloat16)
    return jnp.dot(high_part, triangle_bf, preferred_element_type=jnp.float32) + jnp.dot(
        low_part, triangle_bf, preferred_element_type=jnp.float32
    )


def local_pass(driving, decay_rate, turn_rate):
    modes_here, time_steps = driving.shape
    sub_width = min(128, time_steps)
    offsets = jnp.arange(sub_width, dtype=jnp.float32)
    triangle_bf = (offsets[:, None] <= offsets[None, :]).astype(jnp.bfloat16)
    angles_now = turn_rate[:, None] * offsets[None, :]
    growth = jnp.exp(decay_rate[:, None] * offsets[None, :])
    shrink = jnp.exp(-decay_rate[:, None] * offsets[None, :])
    cosine = jnp.cos(angles_now)
    sine_part = jnp.sin(angles_now)
    rot_real = shrink * cosine
    rot_imag = shrink * sine_part
    ahead_steps = offsets + 1.0
    ahead_angles = turn_rate[:, None] * ahead_steps[None, :]
    ahead_mag = jnp.exp(-decay_rate[:, None] * ahead_steps[None, :])
    ahead_real = ahead_mag * jnp.cos(ahead_angles)
    ahead_imag = ahead_mag * jnp.sin(ahead_angles)
    start_real = jnp.zeros((modes_here,), jnp.float32)
    start_imag = jnp.zeros((modes_here,), jnp.float32)
    pieces = []
    for sub_index in range(time_steps // sub_width):
        segment = driving[:, sub_index * sub_width : (sub_index + 1) * sub_width]
        sum_real = running_sum(segment * growth * cosine, triangle_bf)
        sum_imag = running_sum(-segment * growth * sine_part, triangle_bf)
        state_real = (
            rot_real * sum_real
            - rot_imag * sum_imag
            + ahead_real * start_real[:, None]
            - ahead_imag * start_imag[:, None]
        )
        state_imag = (
            rot_real * sum_imag
            + rot_imag * sum_real
            + ahead_real * start_imag[:, None]
            + ahead_imag * start_real[:, None]
        )
        pieces.append(state_imag)
        start_real = state_real[:, -1]
        start_imag = state_imag[:, -1]
    return (jnp.concatenate(pieces, axis=1), start_real, start_imag)


def respond(forces, decay_rate, turn_rate, prior_part):
    time_steps = forces.shape[1]
    gain = jnp.sqrt(1.0 - jnp.exp(-2.0 * decay_rate))
    imag_local, end_real, end_imag = local_pass(forces * gain[:, None], decay_rate, turn_rate)
    block_mag = jnp.exp(-decay_rate * time_steps)
    block_real = block_mag * jnp.cos(turn_rate * time_steps)
    block_imag = block_mag * jnp.sin(turn_rate * time_steps)
    is_first = lax.axis_index("tm") == 0

    def relay(turn_count, incoming):
        out_real = block_real * incoming[0] - block_imag * incoming[1] + end_real
        out_imag = block_real * incoming[1] + block_imag * incoming[0] + end_imag
        moved = passed_along(jnp.stack([out_real, out_imag]), "tm", 1)
        return jnp.where(is_first, prior_part, moved)

    incoming = lax.fori_loop(
        0, lax.axis_size("tm") - 1, relay, jnp.where(is_first, prior_part, 0.0)
    )
    in_real = incoming[0]
    in_imag = incoming[1]
    ahead = jnp.arange(1, time_steps + 1, dtype=jnp.float32)
    magnitude = jnp.exp(-decay_rate[:, None] * ahead[None, :])
    angles = turn_rate[:, None] * ahead[None, :]
    imaginary = imag_local + magnitude * (
        jnp.sin(angles) * in_real[:, None] + jnp.cos(angles) * in_imag[:, None]
    )
    return imaginary.astype(jnp.bfloat16)


def local(
    wind_speed, span_of_point, drag_factor, mode_shapes, damping, turning, prior_state, recovery
):
    spans_here, time_steps = wind_speed.shape
    half_modes = mode_shapes.shape[1]
    pts_index = lax.axis_index("pts")
    local_span = span_of_point - pts_index * spans_here
    span_ids = jnp.arange(spans_here, dtype=jnp.int32)
    one_hot = (span_ids[:, None] == local_span[None, :]).astype(jnp.bfloat16)
    at_points = lax.dot_general(
        one_hot, wind_speed, (((0,), (0,)), ((), ())), preferred_element_type=jnp.float32
    )
    point_loads = (drag_factor[:, None] * at_points * jnp.abs(at_points)).astype(jnp.bfloat16)
    owned_modes = half_modes // lax.axis_size("pts")
    forces = lax.psum_scatter(
        lax.dot_general(
            mode_shapes, point_loads, (((0,), (0,)), ((), ())), preferred_element_type=jnp.float32
        ).astype(jnp.bfloat16),
        "pts",
        scatter_dimension=0,
        tiled=True,
    ).astype(jnp.float32)
    offset = pts_index * owned_modes
    decay_rate = lax.dynamic_slice_in_dim(damping, offset, owned_modes, 0)
    turn_rate = lax.dynamic_slice_in_dim(turning, offset, owned_modes, 0)
    prior_part = lax.dynamic_slice_in_dim(prior_state, offset, owned_modes, 1)
    response = respond(forces, decay_rate, turn_rate, prior_part)
    partial_value = lax.dot_general(
        lax.all_gather(response, "pts", axis=0, tiled=True),
        recovery,
        (((0,), (0,)), ((), ())),
        preferred_element_type=jnp.float32,
    )
    stress = lax.psum_scatter(
        partial_value.astype(jnp.bfloat16), "rep", scatter_dimension=1, tiled=True
    )
    return stress


def solution(mesh):
    placed = (
        P(("runs", "pts"), "tm"),
        P("pts"),
        P("pts"),
        P("pts", "rep"),
        P("rep"),
        P("rep"),
        P("runs", "rep"),
        P("rep", "pts"),
    )
    return jax.shard_map(
        local,
        mesh=mesh,
        in_specs=placed,
        out_specs=P(("runs", "tm"), ("pts", "rep")),
        check_vma=False,
    )
```

profile of v0, /device:TPU:1, one launch (start us, length us, event | category | flops | bytes accessed | tf_op | source)
XLA Modules:
  0.0 166.0 jit_solution(6543262706333747908)
XLA Ops:
  6.5 0.0 copy-start
  6.5 0.0 reduce-scatter.3.cloned.1.call-start
  6.5 0.8 broadcast_subtract_fusion
  7.4 9.4 %fusion = bf16[2048,512]{0,1:T(8,128)(2,1)} fusion(bf16[2048,2048]{1,0:T(8,128)(2,1)} %param.11, bf16[32,512]{1,0:T(8,128)(2,1)} %param.8, f32[2048]{0:T(1024)} %param.10, s32[2048]{0:T(1024)S(1)} %broadcast_subtract_fusion), kind=kOutput, calls=%fused_computation.2 | convolution fusion | flops 4367384576 | bytes 10534912 | tf_op jit(solution)/shard_map/dot_general | solution.py:107
  16.8 0.0 copy-start.2
  16.8 0.0 copy-start.1
  16.8 0.0 reduce-scatter.3.cloned.1.call-update
  16.8 0.2 all-gather.2.cloned.1.call-start
  17.0 0.4 copy-done.2
  17.5 0.1 dynamic_slice.10
  17.5 0.8 fusion.72
  18.3 0.0 copy-done.1
  18.3 44.4 %reduce-scatter.3.cloned.1.call-done = bf16[512,512]{0,1:T(8,128)(2,1)} async-done(((bf16[2048,512]{0,1:T(8,128)(2,1)}), bf16[512,512]{0,1:T(8,128)(2,1)}) %reduce-scatter.3.cloned.1.call-update) | async-done | bytes 524304 | tf_op jit(solution)/shard_map/reduce_scatter | solution.py:106
  62.7 1.2 convert_multiply_fusion
  63.9 1.3 fusion.48
  65.2 1.3 fusion.47
  66.4 1.3 fusion.46
  67.7 1.3 fusion.45
  69.0 1.3 fusion.44
  70.3 1.3 fusion.43
  71.5 1.3 fusion.42
  72.8 1.3 fusion.41
  74.1 1.3 convolution_add_fusion.7
  75.4 3.0 %fusion.7 = (f32[512,128]{0,1:T(8,128)S(1)}, f32[512,128]{0,1:T(8,128)S(1)}, f32[512,128]{0,1:T(8,128)S(1)}, f32[512,128]{0,1:T(8,128)S(1)}, f32[512,128]{0,1:T(...) fusion(f32[128]{0:T(128)S(1)} %iota_add_fusion.1, f32[512]{0:T(512)S(1)} %dynamic_slice.10, ...), kind=kOutput, calls=%fused_computation.23 | convolution fusion | flops 18366464 | bytes 2892288 | tf_op jit(solution)/shard_map/dot_general | solution.py:16
  78.4 1.3 convolution_add_fusion.5
  79.7 3.0 %multiply_add_fusion.2 = (f32[512,128]{0,1:T(8,128)S(1)}, f32[512,128]{0,1:T(8,128)S(1)}) fusion(f32[512,128]{0,1:T(8,128)S(1)} %convolution_add_fusion.5, f32[512]{0:T(512)S(1)} %bitcast.24, f32[512]{0:T(512)S(1)} %bitcast.31, f32[128]{0:T(128)S(1)} %iota_add_fusion.1, f32[512]{0:T(512)S(1)} %dynamic_slice.10, f32[512]{0:T(512)S(1)} %get-tuple-element.19, ...), kind=kOutput, calls=%fused_computation.35 | convolution fusion | flops 18366464 | bytes 1323520 | tf_op jit(solution)/shard_map/dot_general | solution.py:16
  82.7 1.5 convolution_add_fusion.3
  84.2 3.0 %multiply_add_fusion.1 = (f32[512,128]{0,1:T(8,128)S(1)}, f32[512,128]{0,1:T(8,128)S(1)}) fusion(f32[512,128]{0,1:T(8,128)S(1)} %convolution_add_fusion.3, f32[512]{0:T(512)S(1)} %bitcast.27, f32[512]{0:T(512)S(1)} %bitcast.34, f32[128]{0:T(128)S(1)} %iota_add_fusion.1, f32[512]{0:T(512)S(1)} %dynamic_slice.10, f32[512]{0:T(512)S(1)} %get-tuple-element.19, ...), kind=kOutput, calls=%fused_computation.30 | convolution fusion | flops 18366464 | bytes 1323520 | tf_op jit(solution)/shard_map/dot_general | solution.py:16
  87.3 1.3 convolution_add_fusion.1
  88.5 3.0 %multiply_add_fusion = (f32[512,128]{0,1:T(8,128)S(1)}, f32[512,128]{0,1:T(8,128)S(1)}) fusion(f32[512,128]{0,1:T(8,128)S(1)} %convolution_add_fusion.1, f32[512]{0:T(512)S(1)} %bitcast.22, f32[512]{0:T(512)S(1)} %bitcast.29, f32[128]{0:T(128)S(1)} %iota_add_fusion.1, f32[512]{0:T(512)S(1)} %dynamic_slice.10, f32[512]{0:T(512)S(1)} %get-tuple-element.19, ...), kind=kOutput, calls=%fused_computation.25 | convolution fusion | flops 18366464 | bytes 1323520 | tf_op jit(solution)/shard_map/dot_general | solution.py:16
  91.6 0.1 subtract_add_fusion
  91.7 3.1 %collective-permute-start = (f32[2,512]{1,0:T(2,128)S(1)}, f32[2,512]{1,0:T(2,128)S(1)}, u32[]{:S(2)}, u32[]{:S(2)}) collective-permute-start(f32[2,512]{1,0:T(2,128)S(1)} %pad_maximum_fusion), channel_id=1, source_target_pairs={{0,2},{1,3},{4,6},{5,7},{8,10},{9,11},{12,14},{13,15},{16,18},{17,... | collective-permute-start | bytes 12296 | tf_op jit(solution)/shard_map/while/body/eval_jaxpr/ppermute | solution.py:10
  94.8 0.7 collective-permute-done
  95.6 5.8 %fusion.5 = bf16[512,512]{0,1:T(8,128)(2,1)} fusion(f32[512,128]{0,1:T(8,128)S(1)} %get-tuple-element.49, f32[512,128]{0,1:T(8,128)S(1)} %get-tuple-element.47, f32[512,128]{0,1:T(8,128)S(1)} %get-tuple-element.45, f32[512,128]{0,1:T(8,128)S(1)} %get-tuple-element.32, f32[512]{0:T(512)S(1)} %bitcast.21, f32[512]{0:T(512)S(1)} %bitcast.20, ...), kind=kLoop, calls=%fused_computation.18 | loop fusion | flops 2883584 | bytes 1583104 | tf_op jit(solution)/shard_map/convert_element_type | solution.py:89
  101.3 0.0 all-gather.2.cloned.1.call-update
  101.4 0.0 reduce-scatter.5.cloned.1.call-start
  101.4 47.2 %all-gather.2.cloned.1.call-done = bf16[2048,512]{0,1:T(8,128)(2,1)} async-done(((bf16[512,512]{0,1:T(8,128)(2,1)}), bf16[2048,512]{0,1:T(8,128)(2,1)}) %all-gather.2.cloned.1.call-update) | async-done | bytes 2097168 | tf_op jit(solution)/shard_map/all_gather | solution.py:120
  148.6 0.0 copy-done
  148.6 3.6 %convolution_convert_fusion.1 = bf16[512,512]{1,0:T(8,128)(2,1)} fusion(bf16[2048,512]{0,1:T(8,128)(2,1)} %all-gather.2.cloned.1.call-done, bf16[2048,512]{1,0:T(8,128)(2,1)S(1)} %copy-done), kind=kOutput, calls=%fused_computation.5 | convolution fusion | flops 1074003968 | bytes 4718592 | tf_op jit(solution)/shard_map/dot_general | solution.py:119
  152.2 0.0 reduce-scatter.5.cloned.1.call-update
  152.3 7.2 %reduce-scatter.5.cloned.1.call-done = bf16[512,256]{1,0:T(8,128)(2,1)} async-done(((bf16[512,512]{1,0:T(8,128)(2,1)}), bf16[512,256]{1,0:T(8,128)(2,1)}) %reduce-scatter.5.cloned.1.call-update) | async-done | bytes 262160 | tf_op jit(solution)/shard_map/reduce_scatter | solution.py:125
  (16 shorter events, 0.2 us)
Async XLA Ops:
  6.5 142.1 %copy-start = (bf16[2048,512]{1,0:T(8,128)(2,1)S(1)}, bf16[2048,512]{1,0:T(8,128)(2,1)}, u32[]{:S(2)}) copy-start(bf16[2048,512]{1,0:T(8,128)(2,1)} %param.15) | copy-start | bytes 6291460
  6.5 56.2 %reduce-scatter.3.cloned.1.call-start = ((), (), s32[]{:S(2)}) async-start(), calls=%async_computation.2 | async-start | bytes 2621440 | tf_op jit(solution)/shard_map/reduce_scatter | solution.py:106
  16.8 0.7 copy-start.2
  16.8 1.5 copy-start.1
  16.8 131.8 %all-gather.2.cloned.1.call-start = ((), (), s32[]{:S(2)}) async-start(), calls=%async_computation.3 | async-start | bytes 2621440 | tf_op jit(solution)/shard_map/all_gather | solution.py:120
  91.7 3.8 %collective-permute-start = (f32[2,512]{1,0:T(2,128)S(1)}, f32[2,512]{1,0:T(2,128)S(1)}, u32[]{:S(2)}, u32[]{:S(2)}) collective-permute-start(f32[2,512]{1,0:T(2,128)S(1)} %pad_maximum_fusion), channel_id=1, source_target_pairs={{0,2},{1,3},{4,6},{5,7},{8,10},{9,11},{12,14},{13,15},{16,18},{17,... | collective-permute-start | bytes 12296 | tf_op jit(solution)/shard_map/while/body/eval_jaxpr/ppermute | solution.py:10
  101.4 58.1 %reduce-scatter.5.cloned.1.call-start = ((), (), s32[]{:S(2)}) async-start(), calls=%async_computation.4 | async-start | bytes 786432 | tf_op jit(solution)/shard_map/reduce_scatter | solution.py:125
Sparse Core Ops, SparseCore 0:
  16.9 45.7 reduce-scatter.2
  101.5 47.0 all-gather.1
  152.4 7.0 reduce-scatter.4
where the time goes:
time: 167 us; the launch traced here: 166 us
  waiting for transfers between devices  99.5 us (60%)
  matrix products  40.4 us (24%)
  between operations  13.3 us (8%)
  other arithmetic  8.82 us (5%)
  starting transfers between devices  3.35 us (2%)
    all_gather x1, waiting for transfers between devices, local(): lax.all_gather(response, 'pts', axis=0, tiled=True)  47.2 us
    reduce_scatter x1, waiting for transfers between devices, local(): lax.psum_scatter(lax.dot_general(mode_shapes, point_loads, (((0,), (0,)),...  44.4 us
    dot_general x8, matrix products, running_sum(): jnp.dot(low_part, triangle_bf, preferred_element_type=jnp.float32)  17.3 us
    dot_general x8, matrix products, running_sum(): jnp.dot(high_part, triangle_bf, preferred_element_type=jnp.float32)  10.1 us
    dot_general x1, matrix products, local(): lax.dot_general(mode_shapes, point_loads, (((0,), (0,)), ((), ())), prefe...  9.37 us
    reduce_scatter x1, waiting for transfers between devices, local(): lax.psum_scatter(partial_value.astype(jnp.bfloat16), 'rep', scatter_dimen...  7.2 us
    convert_element_type x1, other arithmetic, respond(): return imaginary.astype(jnp.bfloat16)  5.8 us
    dot_general x1, matrix products, local(): lax.dot_general(lax.all_gather(response, 'pts', axis=0, tiled=True), reco...  3.65 us
  transfers between devices with their start and end apart: 4, of which 4 were waited for; matrix products, arithmetic and copies ran while one was open for 1% of the time, Pallas kernels for 0%

commit v1 on v0

v1 whole, which is shorter than its diff:
```python
import functools

import jax
import jax.numpy as jnp
from jax import lax
from jax.experimental import pallas as pl
from jax.experimental.pallas import tpu as pltpu
from jax.sharding import PartitionSpec as P

CHUNKS = 8
F32 = jnp.float32
BF16 = jnp.bfloat16


def times(a, b):
    return (a[0] * b[0] - a[1] * b[1], a[0] * b[1] + a[1] * b[0])


def power(base, exponent):
    result = None
    while exponent:
        if exponent % 2:
            result = base if result is None else times(result, base)
        exponent //= 2
        if exponent:
            base = times(base, base)
    return result


def remote(src, dst, send_sem, recv_sem, where):
    return pltpu.make_async_remote_copy(
        src_ref=src,
        dst_ref=dst,
        send_sem=send_sem,
        recv_sem=recv_sem,
        device_id=where,
        device_id_type=pl.DeviceIdType.MESH,
    )


def kernel(
    sizes,
    wind_ref, span_ref, drag_ref, shapes_ref, damp_ref, turn_ref, prior_ref, rec_ref,
    out_ref,
    shapes_v, rec_v, winds, bases, forces, ends, entry, coef, resp, part_out, part_in,
    load_sem, wsend, wrecv, zsend, zrecv, xsend, xrecv, esend, erecv, rsend, rrecv,
):
    n_r, n_z, n_t = sizes
    groups = n_r * n_t
    spans, steps = wind_ref.shape
    modes = damp_ref.shape[1]
    width = modes // groups
    length = steps // CHUNKS
    clamps = rec_ref.shape[1]
    half = clamps // 2
    r, z, x, c = (lax.axis_index(a) for a in ("runs", "pts", "tm", "rep"))
    mine = r * n_t + x

    def plane(k, sign=1):
        dr, dx = divmod(k, n_t)
        return lax.rem(r + sign * dr + n_r, n_r), lax.rem(x + sign * dx + n_t, n_t)

    def along_z(o):
        return lax.rem(z + o, n_z)

    barrier = pltpu.get_barrier_semaphore()
    peers = [{"pts": along_z(o)} for o in range(1, n_z)]
    for k in range(1, groups):
        pr, px = plane(k)
        peers.append({"runs": pr, "tm": px})
    peers.append({"rep": 1 - c})
    load_shapes = pltpu.make_async_copy(
        shapes_ref.at[:, pl.ds(pl.multiple_of(mine * width, width), width)], shapes_v, load_sem.at[0]
    )
    load_shapes.start()
    load_rec = pltpu.make_async_copy(rec_ref, rec_v, load_sem.at[1])
    for peer in peers:
        pl.semaphore_signal(barrier, inc=1, device_id=peer, device_id_type=pl.DeviceIdType.MESH)

    span_id = lax.broadcasted_iota(jnp.int32, (spans, span_ref.shape[1]), 0)
    spread = jnp.where(span_id == span_ref[...] - z * spans, drag_ref[...], 0.0)
    spread_hi = spread.astype(BF16)
    spread_lo = (spread - spread_hi.astype(F32)).astype(BF16)
    spread2 = jnp.concatenate([spread_hi, spread_lo], axis=0)
    my_damp = damp_ref[:, pl.ds(pl.multiple_of(mine * width, width), width)]
    gain = jnp.sqrt(1.0 - jnp.exp(-2.0 * my_damp))
    own_rows = pl.ds(pl.multiple_of(z * spans, spans), spans)
    winds[own_rows, :] = wind_ref[...]

    pl.semaphore_wait(barrier, len(peers))
    pending = []
    wind_in = []
    order = sorted(range(1, n_z), key=lambda o: min(o, n_z - o))
    for o in order:
        copy = remote(
            wind_ref, winds.at[own_rows, :], wsend.at[o - 1], wrecv.at[o - 1], {"pts": along_z(o)}
        )
        copy.start()
        pending.append(copy)
        wind_in.append(copy)

    load_shapes.wait()
    load_rec.start()
    base2 = jnp.dot(spread2, shapes_v[...], preferred_element_type=F32)
    base = (base2[:spans] + base2[spans:]) * gain
    bases[mine, own_rows, :] = base.astype(BF16)

    z_in = {}
    for o in order:
        block = bases.at[mine, own_rows, :]
        copy = remote(block, block, zsend.at[o - 1], zrecv.at[o - 1], {"pts": along_z(o)})
        copy.start()
        pending.append(copy)
        z_in[o] = copy

    x_in = {k: [] for k in range(1, groups)}

    def forward(block, piece):
        for k in range(1, groups):
            pr, px = plane(k)
            copy = remote(
                block, block, xsend.at[k - 1, piece], xrecv.at[k - 1, piece], {"runs": pr, "tm": px}
            )
            copy.start()
            pending.append(copy)
            x_in[k].append(copy)

    by_block = n_z <= 4
    if by_block:
        forward(bases.at[mine, own_rows, :], 0)

    for i in range(groups):
        cols = slice(i * width, (i + 1) * width)
        decay = jnp.exp(-damp_ref[:, cols])
        turn = turn_ref[:, cols]
        one = (decay * jnp.cos(turn), decay * jnp.sin(turn))
        chunk = power(one, length)
        block_pow = power(chunk, CHUNKS)
        row = lax.broadcasted_iota(jnp.int32, (CHUNKS, width), 0)
        ahead = (jnp.ones((1, width), F32), jnp.zeros((1, width), F32))
        spread_re = jnp.zeros((CHUNKS, width), F32)
        spread_im = jnp.zeros((CHUNKS, width), F32)
        for s in range(CHUNKS):
            spread_re = jnp.where(row == s, ahead[0], spread_re)
            spread_im = jnp.where(row == s, ahead[1], spread_im)
            ahead = times(ahead, chunk)
        full = jnp.zeros((CHUNKS, width), F32)
        for slot, value in enumerate((*one, *chunk, *block_pow)):
            coef[i, slot] = full + value
        coef[i, 6] = spread_re
        coef[i, 7] = spread_im
    row = lax.broadcasted_iota(jnp.int32, (steps, steps), 0)
    col = lax.broadcasted_iota(jnp.int32, (steps, steps), 1)
    shuffle = (col == (row % CHUNKS) * length + row // CHUNKS).astype(BF16)

    for copy in wind_in:
        copy.wait_recv()
    v = lax.dot_general(shuffle, winds[...], (((1,), (1,)), ((), ())), preferred_element_type=F32)
    q = v * jnp.abs(v)
    q_hi = q.astype(BF16)
    q_lo = (q - q_hi.astype(F32)).astype(BF16)
    q2 = jnp.concatenate([q_hi, q_lo], axis=1)

    for o in order:
        z_in[o].wait_recv()
        if by_block:
            src_rows = pl.ds(pl.multiple_of(lax.rem(z - o + n_z, n_z) * spans, spans), spans)
            forward(bases.at[mine, src_rows, :], o)
    if not by_block:
        forward(bases.at[mine], 0)

    e_in = []
    for k in range(groups):
        pr, px = plane(k, -1)
        group = pr * n_t + px
        if k:
            for copy in x_in[k]:
                copy.wait_recv()
        b = bases[group]
        forces[k] = jnp.dot(q2, jnp.concatenate([b, b], axis=0), preferred_element_type=F32)
        zr, zi = coef[group, 0], coef[group, 1]

        def step(j, state, k=k, zr=zr, zi=zi):
            f = forces[k, pl.ds(pl.multiple_of(j * CHUNKS, CHUNKS), CHUNKS), :]
            return (zr * state[0] - zi * state[1] + f, zr * state[1] + zi * state[0])

        zero = jnp.zeros((CHUNKS, width), F32)
        end_re, end_im = lax.fori_loop(0, length, step, (zero, zero), unroll=8)
        chunk = (coef[group, 2][:1], coef[group, 3][:1])
        row8 = lax.broadcasted_iota(jnp.int32, (CHUNKS, width), 0)
        state = (zero[:1], zero[:1])
        in_re, in_im = zero, zero
        for s in range(CHUNKS):
            if s:
                in_re = jnp.where(row8 == s, state[0], in_re)
                in_im = jnp.where(row8 == s, state[1], in_im)
            moved = times(chunk, state)
            state = (moved[0] + end_re[s : s + 1], moved[1] + end_im[s : s + 1])
        entry[k, 0] = in_re
        entry[k, 1] = in_im
        ends[x, group] = jnp.where(row8 == 0, state[0], state[1])
        arrivals = []
        for dx in range(1, n_t):
            block = ends.at[x, group]
            copy = remote(
                block, block, esend.at[group, dx - 1], erecv.at[group, dx - 1],
                {"tm": lax.rem(x + dx, n_t)},
            )
            copy.start()
            pending.append(copy)
            arrivals.append(copy)
        e_in.append(arrivals)

    for k in range(groups):
        pr, px = plane(k, -1)
        group = pr * n_t + px
        for copy in e_in[k]:
            copy.wait_recv()
        cols = pl.ds(pl.multiple_of(group * width, width), width)
        prior = prior_ref[:, cols]
        state = (prior[:1], prior[1:2])
        block_pow = (coef[group, 4][:1], coef[group, 5][:1])
        for y in range(n_t - 1):
            moved = times(block_pow, state)
            e = ends[y, group]
            state = (
                jnp.where(y < x, moved[0] + e[:1], state[0]),
                jnp.where(y < x, moved[1] + e[1:2], state[1]),
            )
        start = times((coef[group, 6], coef[group, 7]), state)
        start = (start[0] + entry[k, 0], start[1] + entry[k, 1])
        zr, zi = coef[group, 0], coef[group, 1]

        def pair(j, state, k=k, zr=zr, zi=zi, cols=cols):
            imag = []
            f2 = forces[k, pl.ds(pl.multiple_of(j * 2 * CHUNKS, 2 * CHUNKS), 2 * CHUNKS), :]
            for s in range(2):
                f = f2[s * CHUNKS : (s + 1) * CHUNKS]
                state = (zr * state[0] - zi * state[1] + f, zr * state[1] + zi * state[0])
                imag.append(state[1])
            rows = pl.ds(pl.multiple_of(j * 2 * CHUNKS, 2 * CHUNKS), 2 * CHUNKS)
            resp[rows, cols] = jnp.concatenate(imag, axis=0).astype(BF16)
            return state

        lax.fori_loop(0, length // 2, pair, start, unroll=4)

    load_rec.wait()
    theirs = pl.ds(pl.multiple_of((1 - c) * half, half), half)
    ours = pl.ds(pl.multiple_of(c * half, half), half)
    part_out[...] = jnp.dot(resp[...], rec_v[:, theirs], preferred_element_type=F32).astype(BF16)
    swap = remote(part_out, part_in, rsend, rrecv, {"rep": 1 - c})
    swap.start()
    own = jnp.dot(resp[...], rec_v[:, ours], preferred_element_type=F32)
    swap.wait_recv()
    total = (own + part_in[...].astype(F32)).astype(BF16)
    restore = (col == (row % length) * CHUNKS + row // length).astype(BF16)
    out_ref[...] = jnp.dot(restore, total, preferred_element_type=F32).astype(BF16)
    swap.wait_send()
    for copy in pending:
        copy.wait_send()


def local(
    wind_speed, span_of_point, drag_factor, mode_shapes, damping, turning, prior_state, recovery
):
    n_r, n_z, n_t = (lax.axis_size(a) for a in ("runs", "pts", "tm"))
    groups = n_r * n_t
    spans, steps = wind_speed.shape
    points, modes = mode_shapes.shape
    clamps = recovery.shape[1]
    width = modes // groups
    pieces = n_z if n_z <= 4 else 1
    vmem = pl.BlockSpec(memory_space=pltpu.VMEM)
    anywhere = pl.BlockSpec(memory_space=pl.ANY)
    dma = pltpu.SemaphoreType.DMA
    return pl.pallas_call(
        functools.partial(kernel, (n_r, n_z, n_t)),
        out_shape=jax.ShapeDtypeStruct((steps, clamps // 2), BF16),
        in_specs=[vmem, vmem, vmem, anywhere, vmem, vmem, vmem, anywhere],
        out_specs=vmem,
        scratch_shapes=[
            pltpu.VMEM((points, width), BF16),
            pltpu.VMEM((modes, clamps), BF16),
            pltpu.VMEM((n_z * spans, steps), BF16),
            pltpu.VMEM((groups, n_z * spans, width), BF16),
            pltpu.VMEM((groups, steps, width), F32),
            pltpu.VMEM((n_t, groups, CHUNKS, width), F32),
            pltpu.VMEM((groups, 2, CHUNKS, width), F32),
            pltpu.VMEM((groups, 8, CHUNKS, width), F32),
            pltpu.VMEM((steps, modes), BF16),
            pltpu.VMEM((steps, clamps // 2), BF16),
            pltpu.VMEM((steps, clamps // 2), BF16),
            dma((2,)),
            dma((n_z - 1,)),
            dma((n_z - 1,)),
            dma((n_z - 1,)),
            dma((n_z - 1,)),
            dma((groups - 1, pieces)),
            dma((groups - 1, pieces)),
            dma((groups, n_t - 1)),
            dma((groups, n_t - 1)),
            dma,
            dma,
        ],
        compiler_params=pltpu.CompilerParams(
            collective_id=0, has_side_effects=True, vmem_limit_bytes=48 * 1024 * 1024
        ),
    )(
        wind_speed,
        span_of_point.reshape(1, points),
        drag_factor.reshape(1, points),
        mode_shapes,
        damping.reshape(1, modes),
        turning.reshape(1, modes),
        prior_state,
        recovery,
    )


def solution(mesh):
    placed = (
        P(("runs", "pts"), "tm"),
        P("pts"),
        P("pts"),
        P("pts", "rep"),
        P("rep"),
        P("rep"),
        P("runs", "rep"),
        P("rep", "pts"),
    )
    return jax.shard_map(
        local,
        mesh=mesh,
        in_specs=placed,
        out_specs=P(("runs", "tm"), ("pts", "rep")),
        check_vma=False,
    )
```

time: 167 us -> 32.8 us (0.20)
  waiting for transfers between devices: 99.5 us -> 0 us
  matrix products: 40.4 us -> 0 us
  Pallas kernels: 0 us -> 25.8 us
  between operations: 13.3 us -> 0.02 us
  other arithmetic: 8.82 us -> 0 us
  local copies, waits for them, and re-layouts: 0.54 us -> 6.56 us
  starting transfers between devices: 3.35 us -> 0 us
    reduce_scatter x2 -> x0, waiting for transfers between devices: 51.6 us -> none  [the longest x1 44.4 us: local(): lax.psum_scatter(lax.dot_general(mode_shapes, point_loads, (((0,), (0,)),...]
    all_gather x1 -> x0, waiting for transfers between devices: 47.2 us -> none  [local(): lax.all_gather(response, 'pts', axis=0, tiled=True)]
    dot_general x18 -> x0, matrix products: 40.4 us -> none  [the longest x8 17.3 us: running_sum(): jnp.dot(low_part, triangle_bf, preferred_element_type=jnp.float32)]
    pallas_call x0 -> x1, Pallas kernels: none -> 25.8 us  [local(): pl.pallas_call(functools.partial(kernel, (n_r, n_z, n_t)), out_shape=jax....]
    unnamed x6 -> x15, local copies, waits for them, and re-layouts: 0.44 us -> 6.56 us
    convert_element_type x1 -> x0, other arithmetic: 5.8 us -> none  [respond(): return imaginary.astype(jnp.bfloat16)]
    ppermute x1 -> x0, starting transfers between devices: 3.08 us -> none  [passed_along(): return lax.ppermute(shard, axis, pairs)]
  transfers between devices with their start and end apart: 4 -> 0, of which waited for: 4 -> 0; matrix products, arithmetic and copies ran while one was open for 1% -> 0% of each run, Pallas kernels for 0% -> 0%
where the time goes in v1:
time: 32.8 us; the launch traced here: 32.3 us
  Pallas kernels  25.8 us (79%)
  local copies, waits for them, and re-layouts  6.56 us (20%)
    pallas_call x1, Pallas kernels, local(): pl.pallas_call(functools.partial(kernel, (n_r, n_z, n_t)), out_shape=jax....  25.8 us
    unnamed x15, local copies, waits for them, and re-layouts  6.56 us

profile of v1, /device:TPU:1, one launch (start us, length us, event | category | flops | bytes accessed | tf_op | source)
XLA Modules:
  0.0 32.3 jit_solution(4126930627317372956)
XLA Ops:
  0.0 0.0 copy-start
  0.0 1.6 %copy-done = bf16[2048,512]{1,0:T(8,128)(2,1)S(1)} copy-done((bf16[2048,512]{1,0:T(8,128)(2,1)S(1)}, bf16[2048,512]{1,0:T(8,128)(2,1)}, u32[]{:S(2)}) %copy-start) | copy-done | bytes 2097176
  1.6 0.0 copy-start.1
  1.6 0.8 %copy-done.1 = bf16[32,512]{1,0:T(8,128)(2,1)S(1)} copy-done((bf16[32,512]{1,0:T(8,128)(2,1)S(1)}, bf16[32,512]{1,0:T(8,128)(2,1)}, u32[]{:S(2)}) %copy-start.1) | copy-done | bytes 32792
  2.4 0.0 copy-start.2
  2.4 0.7 %copy-done.2 = f32[2,2048]{1,0:T(2,128)S(1)} copy-done((f32[2,2048]{1,0:T(2,128)S(1)}, f32[2,2048]{1,0:T(2,128)}, u32[]{:S(2)}) %copy-start.2) | copy-done | bytes 16408
  3.1 0.0 copy-start.3
  3.1 0.7 %copy-done.3 = s32[2048]{0:T(1024)S(1)} copy-done((s32[2048]{0:T(1024)S(1)}, s32[2048]{0:T(1024)}, u32[]{:S(2)}) %copy-start.3) | copy-done | bytes 8216
  3.8 0.0 copy-start.4
  3.8 0.7 %copy-done.4 = f32[2048]{0:T(1024)S(1)} copy-done((f32[2048]{0:T(1024)S(1)}, f32[2048]{0:T(1024)}, u32[]{:S(2)}) %copy-start.4) | copy-done | bytes 8216
  4.5 0.0 copy-start.5
  4.5 0.7 %copy-done.5 = f32[2048]{0:T(1024)S(1)} copy-done((f32[2048]{0:T(1024)S(1)}, f32[2048]{0:T(1024)}, u32[]{:S(2)}) %copy-start.5) | copy-done | bytes 8216
  5.2 0.0 copy-start.6
  5.2 0.7 %copy-done.6 = f32[2048]{0:T(1024)S(1)} copy-done((f32[2048]{0:T(1024)S(1)}, f32[2048]{0:T(1024)}, u32[]{:S(2)}) %copy-start.6) | copy-done | bytes 8216
  5.9 25.8 %shard_map.82 = bf16[512,256]{1,0:T(8,128)(2,1)S(1)} custom-call(bf16[32,512]{1,0:T(8,128)(2,1)S(1)} %copy-done.1, s32[1,2048]{1,0:T(1,128)S(1)} %bitcast.4, f32[1,2048]{1,0:T(1,128)S(1)} %bitcast.5, bf16[2048,2048]{1,0:T(8,128)(2,1)} %shapes_ref.1, f32[1,2048]{1,0:T(1,128)S(1)} %bitcast.6, f32[1,2048]{1,0:T(1,128)S(1)} %bitcast.7, f32[2,2048]{1,0:T(2,128)S(1)} %copy-done.2, ...), custom_call_target="tpu_custom_call" | custom-call | tf_op jit(solution)/shard_map/pallas_call | solution.py:276
  31.6 0.7 %copy.10 = bf16[512,256]{1,0:T(8,128)(2,1)} copy(bf16[512,256]{1,0:T(8,128)(2,1)S(1)} %shard_map.82) | data formatting | bytes 524288
Async XLA Ops:
  0.0 1.6 %copy-start = (bf16[2048,512]{1,0:T(8,128)(2,1)S(1)}, bf16[2048,512]{1,0:T(8,128)(2,1)}, u32[]{:S(2)}) copy-start(bf16[2048,512]{1,0:T(8,128)(2,1)} %rec_ref.1) | copy-start | bytes 6291460
  1.6 0.8 %copy-start.1 = (bf16[32,512]{1,0:T(8,128)(2,1)S(1)}, bf16[32,512]{1,0:T(8,128)(2,1)}, u32[]{:S(2)}) copy-start(bf16[32,512]{1,0:T(8,128)(2,1)} %wind_ref.1) | copy-start | bytes 98308
  2.4 0.7 %copy-start.2 = (f32[2,2048]{1,0:T(2,128)S(1)}, f32[2,2048]{1,0:T(2,128)}, u32[]{:S(2)}) copy-start(f32[2,2048]{1,0:T(2,128)} %prior_ref.1) | copy-start | bytes 49156
  3.1 0.7 %copy-start.3 = (s32[2048]{0:T(1024)S(1)}, s32[2048]{0:T(1024)}, u32[]{:S(2)}) copy-start(s32[2048]{0:T(1024)} %param.9) | copy-start | bytes 24580
  3.8 0.7 %copy-start.4 = (f32[2048]{0:T(1024)S(1)}, f32[2048]{0:T(1024)}, u32[]{:S(2)}) copy-start(f32[2048]{0:T(1024)} %param.10) | copy-start | bytes 24580
  4.5 0.7 %copy-start.5 = (f32[2048]{0:T(1024)S(1)}, f32[2048]{0:T(1024)}, u32[]{:S(2)}) copy-start(f32[2048]{0:T(1024)} %param.12) | copy-start | bytes 24580
  5.2 0.7 %copy-start.6 = (f32[2048]{0:T(1024)S(1)}, f32[2048]{0:T(1024)}, u32[]{:S(2)}) copy-start(f32[2048]{0:T(1024)} %param.13) | copy-start | bytes 24580

commit v2 on v1

--- a/solution.py
+++ b/solution.py
@@ -40,8 +40,9 @@
 
 def kernel(
     sizes,
-    wind_ref, span_ref, drag_ref, shapes_ref, damp_ref, turn_ref, prior_ref, rec_ref,
+    wind_h, span_h, drag_h, shapes_ref, damp_h, turn_h, prior_h, rec_ref,
     out_ref,
+    wind_ref, span_ref, drag_ref, damp_ref, turn_ref, prior_ref, restore,
     shapes_v, rec_v, winds, bases, forces, ends, entry, coef, resp, part_out, part_in,
     load_sem, wsend, wrecv, zsend, zrecv, xsend, xrecv, esend, erecv, rsend, rrecv,
 ):
@@ -72,11 +73,20 @@
     load_shapes = pltpu.make_async_copy(
         shapes_ref.at[:, pl.ds(pl.multiple_of(mine * width, width), width)], shapes_v, load_sem.at[0]
     )
+    small = []
+    for i, (src, dst) in enumerate((
+        (span_h, span_ref), (drag_h, drag_ref), (damp_h, damp_ref),
+        (wind_h, wind_ref), (turn_h, turn_ref), (prior_h, prior_ref),
+    )):
+        small.append(pltpu.make_async_copy(src, dst, load_sem.at[2 + i]))
+        small[-1].start()
     load_shapes.start()
     load_rec = pltpu.make_async_copy(rec_ref, rec_v, load_sem.at[1])
     for peer in peers:
         pl.semaphore_signal(barrier, inc=1, device_id=peer, device_id_type=pl.DeviceIdType.MESH)
 
+    for copy in small[:3]:
+        copy.wait()
     span_id = lax.broadcasted_iota(jnp.int32, (spans, span_ref.shape[1]), 0)
     spread = jnp.where(span_id == span_ref[...] - z * spans, drag_ref[...], 0.0)
     spread_hi = spread.astype(BF16)
@@ -85,6 +95,7 @@
     my_damp = damp_ref[:, pl.ds(pl.multiple_of(mine * width, width), width)]
     gain = jnp.sqrt(1.0 - jnp.exp(-2.0 * my_damp))
     own_rows = pl.ds(pl.multiple_of(z * spans, spans), spans)
+    small[3].wait()
     winds[own_rows, :] = wind_ref[...]
 
     pl.semaphore_wait(barrier, len(peers))
@@ -129,6 +140,8 @@
     if by_block:
         forward(bases.at[mine, own_rows, :], 0)
 
+    small[4].wait()
+    small[5].wait()
     for i in range(groups):
         cols = slice(i * width, (i + 1) * width)
         decay = jnp.exp(-damp_ref[:, cols])
@@ -151,7 +164,9 @@
         coef[i, 7] = spread_im
     row = lax.broadcasted_iota(jnp.int32, (steps, steps), 0)
     col = lax.broadcasted_iota(jnp.int32, (steps, steps), 1)
-    shuffle = (col == (row % CHUNKS) * length + row // CHUNKS).astype(BF16)
+    low, shift = CHUNKS - 1, CHUNKS.bit_length() - 1
+    shuffle = (col == (row & low) * length + (row >> shift)).astype(BF16)
+    restore[...] = (row == (col & low) * length + (col >> shift)).astype(BF16)
 
     for copy in wind_in:
         copy.wait_recv()
@@ -253,8 +268,7 @@
     own = jnp.dot(resp[...], rec_v[:, ours], preferred_element_type=F32)
     swap.wait_recv()
     total = (own + part_in[...].astype(F32)).astype(BF16)
-    restore = (col == (row % length) * CHUNKS + row // length).astype(BF16)
-    out_ref[...] = jnp.dot(restore, total, preferred_element_type=F32).astype(BF16)
+    out_ref[...] = jnp.dot(restore[...], total, preferred_element_type=F32).astype(BF16)
     swap.wait_send()
     for copy in pending:
         copy.wait_send()
@@ -271,14 +285,21 @@
     width = modes // groups
     pieces = n_z if n_z <= 4 else 1
     vmem = pl.BlockSpec(memory_space=pltpu.VMEM)
-    anywhere = pl.BlockSpec(memory_space=pl.ANY)
+    hbm = pl.BlockSpec(memory_space=pltpu.HBM)
     dma = pltpu.SemaphoreType.DMA
     return pl.pallas_call(
         functools.partial(kernel, (n_r, n_z, n_t)),
         out_shape=jax.ShapeDtypeStruct((steps, clamps // 2), BF16),
-        in_specs=[vmem, vmem, vmem, anywhere, vmem, vmem, vmem, anywhere],
+        in_specs=[hbm] * 8,
         out_specs=vmem,
         scratch_shapes=[
+            pltpu.VMEM((spans, steps), BF16),
+            pltpu.VMEM((1, points), jnp.int32),
+            pltpu.VMEM((1, points), F32),
+            pltpu.VMEM((1, modes), F32),
+            pltpu.VMEM((1, modes), F32),
+            pltpu.VMEM((2, modes), F32),
+            pltpu.VMEM((steps, steps), BF16),
             pltpu.VMEM((points, width), BF16),
             pltpu.VMEM((modes, clamps), BF16),
             pltpu.VMEM((n_z * spans, steps), BF16),
@@ -290,7 +311,7 @@
             pltpu.VMEM((steps, modes), BF16),
             pltpu.VMEM((steps, clamps // 2), BF16),
             pltpu.VMEM((steps, clamps // 2), BF16),
-            dma((2,)),
+            dma((8,)),
             dma((n_z - 1,)),
             dma((n_z - 1,)),
             dma((n_z - 1,)),
@@ -303,7 +324,7 @@
             dma,
         ],
         compiler_params=pltpu.CompilerParams(
-            collective_id=0, has_side_effects=True, vmem_limit_bytes=48 * 1024 * 1024
+            collective_id=0, has_side_effects=True, vmem_limit_bytes=64 * 1024 * 1024
         ),
     )(
         wind_speed,

time: 32.8 us -> 28.4 us (0.87)
  local copies, waits for them, and re-layouts: 6.56 us -> 1.67 us
  Pallas kernels: 25.8 us -> 26.5 us
    unnamed x15 -> x1, local copies, waits for them, and re-layouts: 6.56 us -> 1.67 us
    pallas_call x1, Pallas kernels: 25.8 us -> 26.5 us  [local(): pl.pallas_call(functools.partial(kernel, (n_r, n_z, n_t)), out_shape=jax....]
where the time goes in v2:
time: 28.4 us; the launch traced here: 28.2 us
  Pallas kernels  26.5 us (93%)
  local copies, waits for them, and re-layouts  1.67 us (6%)
    pallas_call x1, Pallas kernels, local(): pl.pallas_call(functools.partial(kernel, (n_r, n_z, n_t)), out_shape=jax....  26.5 us
    unnamed x1, local copies, waits for them, and re-layouts  1.67 us

profile of v2, /device:TPU:1, one launch (start us, length us, event | category | flops | bytes accessed | tf_op | source)
XLA Modules:
  0.0 28.2 jit_solution(12101320047381419620)
XLA Ops:
  0.0 26.5 %shard_map.82 = bf16[512,256]{1,0:T(8,128)(2,1)} custom-call(bf16[32,512]{1,0:T(8,128)(2,1)} %wind_h.1, s32[1,2048]{1,0:T(1,128)} %bitcast.4, f32[1,2048]{1,0:T(1,128)} %bitcast.5, bf16[2048,2048]{1,0:T(8,128)(2,1)} %shapes_ref.1, f32[1,2048]{1,0:T(1,128)} %bitcast.6, f32[1,2048]{1,0:T(1,128)} %bitcast.7, f32[2,2048]{1,0:T(2,128)} %prior_h.1, ...), custom_call_target="tpu_custom_call" | custom-call | tf_op jit(solution)/shard_map/pallas_call | solution.py:290
  26.5 1.7 %copy.10 = bf16[512,256]{1,0:T(8,128)(2,1)} copy(bf16[512,256]{1,0:T(8,128)(2,1)} %shard_map.82) | data formatting | bytes 524288

commit v3 on v2

--- a/solution.py
+++ b/solution.py
@@ -43,7 +43,7 @@
     wind_h, span_h, drag_h, shapes_ref, damp_h, turn_h, prior_h, rec_ref,
     out_ref,
     wind_ref, span_ref, drag_ref, damp_ref, turn_ref, prior_ref, restore,
-    shapes_v, rec_v, winds, bases, forces, ends, entry, coef, resp, part_out, part_in,
+    shapes_v, rec_v, winds, bases, forces, ends, entry, coef, resp, partial, part_out, part_in,
     load_sem, wsend, wrecv, zsend, zrecv, xsend, xrecv, esend, erecv, rsend, rrecv,
 ):
     n_r, n_z, n_t = sizes
@@ -97,48 +97,6 @@
     own_rows = pl.ds(pl.multiple_of(z * spans, spans), spans)
     small[3].wait()
     winds[own_rows, :] = wind_ref[...]
-
-    pl.semaphore_wait(barrier, len(peers))
-    pending = []
-    wind_in = []
-    order = sorted(range(1, n_z), key=lambda o: min(o, n_z - o))
-    for o in order:
-        copy = remote(
-            wind_ref, winds.at[own_rows, :], wsend.at[o - 1], wrecv.at[o - 1], {"pts": along_z(o)}
-        )
-        copy.start()
-        pending.append(copy)
-        wind_in.append(copy)
-
-    load_shapes.wait()
-    load_rec.start()
-    base2 = jnp.dot(spread2, shapes_v[...], preferred_element_type=F32)
-    base = (base2[:spans] + base2[spans:]) * gain
-    bases[mine, own_rows, :] = base.astype(BF16)
-
-    z_in = {}
-    for o in order:
-        block = bases.at[mine, own_rows, :]
-        copy = remote(block, block, zsend.at[o - 1], zrecv.at[o - 1], {"pts": along_z(o)})
-        copy.start()
-        pending.append(copy)
-        z_in[o] = copy
-
-    x_in = {k: [] for k in range(1, groups)}
-
-    def forward(block, piece):
-        for k in range(1, groups):
-            pr, px = plane(k)
-            copy = remote(
-                block, block, xsend.at[k - 1, piece], xrecv.at[k - 1, piece], {"runs": pr, "tm": px}
-            )
-            copy.start()
-            pending.append(copy)
-            x_in[k].append(copy)
-
-    by_block = n_z <= 4
-    if by_block:
-        forward(bases.at[mine, own_rows, :], 0)
 
     small[4].wait()
     small[5].wait()
@@ -168,6 +126,56 @@
     shuffle = (col == (row & low) * length + (row >> shift)).astype(BF16)
     restore[...] = (row == (col & low) * length + (col >> shift)).astype(BF16)
 
+    load_shapes.wait()
+    load_rec.start()
+    base2 = jnp.dot(spread2, shapes_v[...], preferred_element_type=F32)
+    base = (base2[:spans] + base2[spans:]) * gain
+    bases[mine, own_rows, :] = base.astype(BF16)
+
+    pl.semaphore_wait(barrier, len(peers))
+    pending = []
+    order = sorted(range(1, n_z), key=lambda o: min(o, n_z - o))
+    z_in = {}
+    for o in order:
+        block = bases.at[mine, own_rows, :]
+        copy = remote(block, block, zsend.at[o - 1], zrecv.at[o - 1], {"pts": along_z(o)})
+        copy.start()
+        pending.append(copy)
+        z_in[o] = copy
+
+    x_in = {k: [] for k in range(1, groups)}
+
+    def forward(block, piece):
+        for k in range(1, groups):
+            pr, px = plane(k)
+            copy = remote(
+                block, block, xsend.at[k - 1, piece], xrecv.at[k - 1, piece], {"runs": pr, "tm": px}
+            )
+            copy.start()
+            pending.append(copy)
+            x_in[k].append(copy)
+
+    by_block = n_z <= 4
+    if by_block:
+        forward(bases.at[mine, own_rows, :], 0)
+
+    wind_in = []
+    for o in order:
+        copy = remote(
+            wind_ref, winds.at[own_rows, :], wsend.at[o - 1], wrecv.at[o - 1], {"pts": along_z(o)}
+        )
+        copy.start()
+        pending.append(copy)
+        wind_in.append(copy)
+
+    for o in order:
+        z_in[o].wait_recv()
+        if by_block:
+            src_rows = pl.ds(pl.multiple_of(lax.rem(z - o + n_z, n_z) * spans, spans), spans)
+            forward(bases.at[mine, src_rows, :], o)
+    if not by_block:
+        forward(bases.at[mine], 0)
+
     for copy in wind_in:
         copy.wait_recv()
     v = lax.dot_general(shuffle, winds[...], (((1,), (1,)), ((), ())), preferred_element_type=F32)
@@ -176,16 +184,9 @@
     q_lo = (q - q_hi.astype(F32)).astype(BF16)
     q2 = jnp.concatenate([q_hi, q_lo], axis=1)
 
-    for o in order:
-        z_in[o].wait_recv()
-        if by_block:
-            src_rows = pl.ds(pl.multiple_of(lax.rem(z - o + n_z, n_z) * spans, spans), spans)
-            forward(bases.at[mine, src_rows, :], o)
-    if not by_block:
-        forward(bases.at[mine], 0)
-
     e_in = []
-    for k in range(groups):
+
+    def first_pass(k):
         pr, px = plane(k, -1)
         group = pr * n_t + px
         if k:
@@ -226,7 +227,7 @@
             arrivals.append(copy)
         e_in.append(arrivals)
 
-    for k in range(groups):
+    def second_pass(k):
         pr, px = plane(k, -1)
         group = pr * n_t + px
         for copy in e_in[k]:
@@ -258,14 +259,33 @@
             return state
 
         lax.fori_loop(0, length // 2, pair, start, unroll=4)
-
-    load_rec.wait()
+        return cols
+
     theirs = pl.ds(pl.multiple_of((1 - c) * half, half), half)
     ours = pl.ds(pl.multiple_of(c * half, half), half)
-    part_out[...] = jnp.dot(resp[...], rec_v[:, theirs], preferred_element_type=F32).astype(BF16)
+    ahead = 0
+    for k in range(groups):
+        due = min(groups, max(k + 2, (k // n_t + 1) * n_t))
+        for j in range(ahead, due):
+            first_pass(j)
+        ahead = due
+        if k == groups - 1:
+            break
+        cols = second_pass(k)
+        if k == 0:
+            load_rec.wait()
+        product = jnp.dot(resp[:, cols], rec_v[cols, :], preferred_element_type=F32)
+        if k:
+            partial[...] += product
+        else:
+            partial[...] = product
+    cols = second_pass(groups - 1)
+    last = jnp.dot(resp[:, cols], rec_v[cols, theirs], preferred_element_type=F32)
+    part_out[...] = (partial[:, theirs] + last).astype(BF16)
     swap = remote(part_out, part_in, rsend, rrecv, {"rep": 1 - c})
     swap.start()
-    own = jnp.dot(resp[...], rec_v[:, ours], preferred_element_type=F32)
+    last = jnp.dot(resp[:, cols], rec_v[cols, ours], preferred_element_type=F32)
+    own = partial[:, ours] + last
     swap.wait_recv()
     total = (own + part_in[...].astype(F32)).astype(BF16)
     out_ref[...] = jnp.dot(restore[...], total, preferred_element_type=F32).astype(BF16)
@@ -309,6 +329,7 @@
             pltpu.VMEM((groups, 2, CHUNKS, width), F32),
             pltpu.VMEM((groups, 8, CHUNKS, width), F32),
             pltpu.VMEM((steps, modes), BF16),
+            pltpu.VMEM((steps, clamps), F32),
             pltpu.VMEM((steps, clamps // 2), BF16),
             pltpu.VMEM((steps, clamps // 2), BF16),
             dma((8,)),

time: 28.4 us -> 29.6 us (1.042)
  Pallas kernels: 26.5 us -> 27.7 us
    pallas_call x1, Pallas kernels: 26.5 us -> 27.7 us  [local(): pl.pallas_call(functools.partial(kernel, (n_r, n_z, n_t)), out_shape=jax....]
where the time goes in v3:
time: 29.6 us; the launch traced here: 29.4 us
  Pallas kernels  27.7 us (94%)
  local copies, waits for them, and re-layouts  1.67 us (6%)
    pallas_call x1, Pallas kernels, local(): pl.pallas_call(functools.partial(kernel, (n_r, n_z, n_t)), out_shape=jax....  27.7 us
    unnamed x1, local copies, waits for them, and re-layouts  1.67 us

profile of v3, /device:TPU:1, one launch (start us, length us, event | category | flops | bytes accessed | tf_op | source)
XLA Modules:
  0.0 29.4 jit_solution(15319397501477954000)
XLA Ops:
  0.0 27.7 %shard_map.82 = bf16[512,256]{1,0:T(8,128)(2,1)} custom-call(bf16[32,512]{1,0:T(8,128)(2,1)} %wind_h.1, s32[1,2048]{1,0:T(1,128)} %bitcast.4, f32[1,2048]{1,0:T(1,128)} %bitcast.5, bf16[2048,2048]{1,0:T(8,128)(2,1)} %shapes_ref.1, f32[1,2048]{1,0:T(1,128)} %bitcast.6, f32[1,2048]{1,0:T(1,128)} %bitcast.7, f32[2,2048]{1,0:T(2,128)} %prior_h.1, ...), custom_call_target="tpu_custom_call" | custom-call | tf_op jit(solution)/shard_map/pallas_call | solution.py:310
  27.7 1.7 %copy.10 = bf16[512,256]{1,0:T(8,128)(2,1)} copy(bf16[512,256]{1,0:T(8,128)(2,1)} %shard_map.82) | data formatting | bytes 524288

commit v4 on v2

--- a/solution.py
+++ b/solution.py
@@ -43,7 +43,7 @@
     wind_h, span_h, drag_h, shapes_ref, damp_h, turn_h, prior_h, rec_ref,
     out_ref,
     wind_ref, span_ref, drag_ref, damp_ref, turn_ref, prior_ref, restore,
-    shapes_v, rec_v, winds, bases, forces, ends, entry, coef, resp, part_out, part_in,
+    shapes_v, rec_v, winds, bases, forces, ends, entry, coef, resp, partial, part_out, part_in,
     load_sem, wsend, wrecv, zsend, zrecv, xsend, xrecv, esend, erecv, rsend, rrecv,
 ):
     n_r, n_z, n_t = sizes
@@ -98,24 +98,15 @@
     small[3].wait()
     winds[own_rows, :] = wind_ref[...]
 
-    pl.semaphore_wait(barrier, len(peers))
-    pending = []
-    wind_in = []
-    order = sorted(range(1, n_z), key=lambda o: min(o, n_z - o))
-    for o in order:
-        copy = remote(
-            wind_ref, winds.at[own_rows, :], wsend.at[o - 1], wrecv.at[o - 1], {"pts": along_z(o)}
-        )
-        copy.start()
-        pending.append(copy)
-        wind_in.append(copy)
-
     load_shapes.wait()
     load_rec.start()
     base2 = jnp.dot(spread2, shapes_v[...], preferred_element_type=F32)
     base = (base2[:spans] + base2[spans:]) * gain
     bases[mine, own_rows, :] = base.astype(BF16)
 
+    pl.semaphore_wait(barrier, len(peers))
+    pending = []
+    order = sorted(range(1, n_z), key=lambda o: min(o, n_z - o))
     z_in = {}
     for o in order:
         block = bases.at[mine, own_rows, :]
@@ -139,6 +130,23 @@
     by_block = n_z <= 4
     if by_block:
         forward(bases.at[mine, own_rows, :], 0)
+
+    wind_in = []
+    for o in order:
+        copy = remote(
+            wind_ref, winds.at[own_rows, :], wsend.at[o - 1], wrecv.at[o - 1], {"pts": along_z(o)}
+        )
+        copy.start()
+        pending.append(copy)
+        wind_in.append(copy)
+
+    for o in order:
+        z_in[o].wait_recv()
+        if by_block:
+            src_rows = pl.ds(pl.multiple_of(lax.rem(z - o + n_z, n_z) * spans, spans), spans)
+            forward(bases.at[mine, src_rows, :], o)
+    if not by_block:
+        forward(bases.at[mine], 0)
 
     small[4].wait()
     small[5].wait()
@@ -176,16 +184,10 @@
     q_lo = (q - q_hi.astype(F32)).astype(BF16)
     q2 = jnp.concatenate([q_hi, q_lo], axis=1)
 
-    for o in order:
-        z_in[o].wait_recv()
-        if by_block:
-            src_rows = pl.ds(pl.multiple_of(lax.rem(z - o + n_z, n_z) * spans, spans), spans)
-            forward(bases.at[mine, src_rows, :], o)
-    if not by_block:
-        forward(bases.at[mine], 0)
-
     e_in = []
-    for k in range(groups):
+    sent_ends = []
+
+    def first_pass(k):
         pr, px = plane(k, -1)
         group = pr * n_t + px
         if k:
@@ -221,16 +223,16 @@
                 block, block, esend.at[group, dx - 1], erecv.at[group, dx - 1],
                 {"tm": lax.rem(x + dx, n_t)},
             )
-            copy.start()
-            pending.append(copy)
-            arrivals.append(copy)
+            pl.when(x + dx < n_t)(copy.start)
+            sent_ends.append((dx, copy))
+            arrivals.append((dx, copy))
         e_in.append(arrivals)
 
-    for k in range(groups):
+    def second_pass(k):
         pr, px = plane(k, -1)
         group = pr * n_t + px
-        for copy in e_in[k]:
-            copy.wait_recv()
+        for dx, copy in e_in[k]:
+            pl.when(x >= dx)(copy.wait_recv)
         cols = pl.ds(pl.multiple_of(group * width, width), width)
         prior = prior_ref[:, cols]
         state = (prior[:1], prior[1:2])
@@ -258,20 +260,36 @@
             return state
 
         lax.fori_loop(0, length // 2, pair, start, unroll=4)
-
-    load_rec.wait()
+        return cols
+
     theirs = pl.ds(pl.multiple_of((1 - c) * half, half), half)
     ours = pl.ds(pl.multiple_of(c * half, half), half)
-    part_out[...] = jnp.dot(resp[...], rec_v[:, theirs], preferred_element_type=F32).astype(BF16)
+    for k in range(groups):
+        first_pass(k)
+    load_rec.wait()
+    turns = list(range(groups))
+    for i, k in enumerate(turns[:-1]):
+        cols = second_pass(k)
+        product = jnp.dot(resp[:, cols], rec_v[cols, :], preferred_element_type=F32)
+        if i:
+            partial[...] += product
+        else:
+            partial[...] = product
+    cols = second_pass(turns[-1])
+    last = jnp.dot(resp[:, cols], rec_v[cols, theirs], preferred_element_type=F32)
+    part_out[...] = (partial[:, theirs] + last).astype(BF16)
     swap = remote(part_out, part_in, rsend, rrecv, {"rep": 1 - c})
     swap.start()
-    own = jnp.dot(resp[...], rec_v[:, ours], preferred_element_type=F32)
+    last = jnp.dot(resp[:, cols], rec_v[cols, ours], preferred_element_type=F32)
+    own = partial[:, ours] + last
     swap.wait_recv()
     total = (own + part_in[...].astype(F32)).astype(BF16)
     out_ref[...] = jnp.dot(restore[...], total, preferred_element_type=F32).astype(BF16)
     swap.wait_send()
     for copy in pending:
         copy.wait_send()
+    for dx, copy in sent_ends:
+        pl.when(x + dx < n_t)(copy.wait_send)
 
 
 def local(
@@ -309,6 +327,7 @@
             pltpu.VMEM((groups, 2, CHUNKS, width), F32),
             pltpu.VMEM((groups, 8, CHUNKS, width), F32),
             pltpu.VMEM((steps, modes), BF16),
+            pltpu.VMEM((steps, clamps), F32),
             pltpu.VMEM((steps, clamps // 2), BF16),
             pltpu.VMEM((steps, clamps // 2), BF16),
             dma((8,)),

time: 28.4 us -> 24.2 us (0.85)
  Pallas kernels: 26.5 us -> 22.2 us
    pallas_call x1, Pallas kernels: 26.5 us -> 22.2 us  [local(): pl.pallas_call(functools.partial(kernel, (n_r, n_z, n_t)), out_shape=jax....]
where the time goes in v4:
time: 24.2 us; the launch traced here: 23.8 us
  Pallas kernels  22.2 us (92%)
  local copies, waits for them, and re-layouts  1.67 us (7%)
    pallas_call x1, Pallas kernels, local(): pl.pallas_call(functools.partial(kernel, (n_r, n_z, n_t)), out_shape=jax....  22.2 us
    unnamed x1, local copies, waits for them, and re-layouts  1.67 us

profile of v4, /device:TPU:1, one launch (start us, length us, event | category | flops | bytes accessed | tf_op | source)
XLA Modules:
  0.0 23.8 jit_solution(15921361950084819507)
XLA Ops:
  0.0 22.2 %shard_map.82 = bf16[512,256]{1,0:T(8,128)(2,1)} custom-call(bf16[32,512]{1,0:T(8,128)(2,1)} %wind_h.1, s32[1,2048]{1,0:T(1,128)} %bitcast.4, f32[1,2048]{1,0:T(1,128)} %bitcast.5, bf16[2048,2048]{1,0:T(8,128)(2,1)} %shapes_ref.1, f32[1,2048]{1,0:T(1,128)} %bitcast.6, f32[1,2048]{1,0:T(1,128)} %bitcast.7, f32[2,2048]{1,0:T(2,128)} %prior_h.1, ...), custom_call_target="tpu_custom_call" | custom-call | tf_op jit(solution)/shard_map/pallas_call | solution.py:308
  22.2 1.7 %copy.10 = bf16[512,256]{1,0:T(8,128)(2,1)} copy(bf16[512,256]{1,0:T(8,128)(2,1)} %shard_map.82) | data formatting | bytes 524288

commit v5 on v4

--- a/solution.py
+++ b/solution.py
@@ -73,6 +73,7 @@
     load_shapes = pltpu.make_async_copy(
         shapes_ref.at[:, pl.ds(pl.multiple_of(mine * width, width), width)], shapes_v, load_sem.at[0]
     )
+    load_shapes.start()
     small = []
     for i, (src, dst) in enumerate((
         (span_h, span_ref), (drag_h, drag_ref), (damp_h, damp_ref),
@@ -80,7 +81,6 @@
     )):
         small.append(pltpu.make_async_copy(src, dst, load_sem.at[2 + i]))
         small[-1].start()
-    load_shapes.start()
     load_rec = pltpu.make_async_copy(rec_ref, rec_v, load_sem.at[1])
     for peer in peers:
         pl.semaphore_signal(barrier, inc=1, device_id=peer, device_id_type=pl.DeviceIdType.MESH)
@@ -115,6 +115,15 @@
         pending.append(copy)
         z_in[o] = copy
 
+    wind_in = []
+    for o in order:
+        copy = remote(
+            wind_ref, winds.at[own_rows, :], wsend.at[o - 1], wrecv.at[o - 1], {"pts": along_z(o)}
+        )
+        copy.start()
+        pending.append(copy)
+        wind_in.append(copy)
+
     x_in = {k: [] for k in range(1, groups)}
 
     def forward(block, piece):
@@ -130,15 +139,6 @@
     by_block = n_z <= 4
     if by_block:
         forward(bases.at[mine, own_rows, :], 0)
-
-    wind_in = []
-    for o in order:
-        copy = remote(
-            wind_ref, winds.at[own_rows, :], wsend.at[o - 1], wrecv.at[o - 1], {"pts": along_z(o)}
-        )
-        copy.start()
-        pending.append(copy)
-        wind_in.append(copy)
 
     for o in order:
         z_in[o].wait_recv()

time: 24.2 us -> 24.1 us (level)
  no operation moved by 1% of the time
where the time goes in v5:
time: 24.1 us; the launch traced here: 23.7 us
  Pallas kernels  22.1 us (92%)
  local copies, waits for them, and re-layouts  1.67 us (7%)
    pallas_call x1, Pallas kernels, local(): pl.pallas_call(functools.partial(kernel, (n_r, n_z, n_t)), out_shape=jax....  22.1 us
    unnamed x1, local copies, waits for them, and re-layouts  1.67 us

profile of v5, /device:TPU:1, one launch (start us, length us, event | category | flops | bytes accessed | tf_op | source)
XLA Modules:
  0.0 23.7 jit_solution(9782781440128213505)
XLA Ops:
  0.0 22.1 %shard_map.82 = bf16[512,256]{1,0:T(8,128)(2,1)} custom-call(bf16[32,512]{1,0:T(8,128)(2,1)} %wind_h.1, s32[1,2048]{1,0:T(1,128)} %bitcast.4, f32[1,2048]{1,0:T(1,128)} %bitcast.5, bf16[2048,2048]{1,0:T(8,128)(2,1)} %shapes_ref.1, f32[1,2048]{1,0:T(1,128)} %bitcast.6, f32[1,2048]{1,0:T(1,128)} %bitcast.7, f32[2,2048]{1,0:T(2,128)} %prior_h.1, ...), custom_call_target="tpu_custom_call" | custom-call | tf_op jit(solution)/shard_map/pallas_call | solution.py:308
  22.1 1.7 %copy.10 = bf16[512,256]{1,0:T(8,128)(2,1)} copy(bf16[512,256]{1,0:T(8,128)(2,1)} %shard_map.82) | data formatting | bytes 524288
